TPU v7x, 32 devices: a whole 2x2x4 slice. The times are simulated.
32 devices in a mesh: dp: 8 (over z, core), ctx: 4 (over y, x).
Axes of the slice: x: 2, y: 2, z: 4, core: 2. Of those that a mesh axis runs over, the one named last changes fastest.
Arguments:
- q_rows: bfloat16 [16384, 2048], P(('dp', 'ctx')), may hold values from -8 to 8
- kv_rows: bfloat16 [16384, 1024], P(('dp', 'ctx')), may hold values from -8 to 8
- packed_slot: int32 [16384], P(('dp', 'ctx')), may hold values from 0 to 16383, as said below
- doc_ids: int32 [8, 2048], P('dp', 'ctx'), may hold values from 0 to 5, never falling along the last dimension, each value on 1 to 1024 neighbouring positions
Outputs:
- attended: bfloat16 [16384, 2048], P(('dp', 'ctx'))
Inputs may be any that keep to these rules, and one draw needn't show every extreme that they name: `packed_slot`: A permutation of the packed positions; the 512 loader rows of every device send exactly 16 rows to the packed positions of each device, position p lying on device p // 512 in the order of dp+ctx. `doc_ids`: document numbers never fall along a sequence; a document has 1 to 1024 positions.
All inputs are finite; a program needn't handle non-finite values.
Results may differ from a plain program's by a relative error of at most 0.0038.
Values may be sent and summed in bfloat16 or wider, within the bound.
No kernel may reach another device: no remote copies, remote signals or barrier semaphores. Data moves between devices by JAX's collectives and lax.ppermute only.
A program may use at most 192 MiB of HBM per device.

v0:
```python
import jax
import jax.numpy as jnp
from jax import lax
from jax.sharding import PartitionSpec as P

HEADS = 16
KV_HEADS = 4
HD = 128
GROUP = 4


neg_big = -1e30


def arrange(q_rows, kv_rows, packed_slot):
    row_count = q_rows.shape[0]
    dp_size = lax.axis_size("dp")
    ctx_size = lax.axis_size("ctx")
    device_count = dp_size * ctx_size
    per_peer = row_count // device_count
    target_dev = packed_slot // row_count
    one_hot = (target_dev[:, None] == jnp.arange(device_count, dtype=jnp.int32)[None, :]).astype(
        jnp.int32
    )
    rank_in = jnp.sum((jnp.cumsum(one_hot, axis=0) - 1) * one_hot, axis=1)
    where_to = target_dev * per_peer + rank_in
    send_order = (
        jnp.zeros((row_count,), jnp.int32).at[where_to].set(jnp.arange(row_count, dtype=jnp.int32))
    )
    q_send = q_rows[send_order]
    kv_send = kv_rows[send_order]
    slot_send = packed_slot[send_order]
    got_q, got_kv, got_slot = (
        lax.all_to_all(q_send, ("dp", "ctx"), split_axis=0, concat_axis=0, tiled=True),
        lax.all_to_all(kv_send, ("dp", "ctx"), split_axis=0, concat_axis=0, tiled=True),
        lax.all_to_all(slot_send, ("dp", "ctx"), split_axis=0, concat_axis=0, tiled=True),
    )
    local_slot = got_slot % row_count
    inverse = (
        jnp.zeros((row_count,), jnp.int32)
        .at[local_slot]
        .set(jnp.arange(row_count, dtype=jnp.int32))
    )
    return (got_q[inverse], got_kv[inverse])


def per_device(q_rows, kv_rows, packed_slot, doc_ids):
    q_here, kv_here = arrange(q_rows, kv_rows, packed_slot)
    row_count = q_here.shape[0]
    inv_scale = 1.0 / jnp.sqrt(jnp.float32(HD))
    query_docs = doc_ids.reshape(row_count)
    query_pos = lax.axis_index("ctx") * row_count + jnp.arange(row_count, dtype=jnp.int32)
    queries = q_here.reshape(row_count, KV_HEADS, GROUP, HD).transpose(1, 2, 0, 3)
    kv_block = lax.all_gather(kv_here, "ctx", axis=0, tiled=True)
    doc_block = lax.all_gather(query_docs, "ctx", axis=0, tiled=True)
    width = kv_block.shape[0]
    key_pos = jnp.arange(width, dtype=jnp.int32)
    allowed = (query_docs[:, None] == doc_block[None, :]) & (key_pos[None, :] <= query_pos[:, None])
    keys = kv_block[:, : KV_HEADS * HD].reshape(width, KV_HEADS, HD).transpose(1, 0, 2)
    values = kv_block[:, KV_HEADS * HD :].reshape(width, KV_HEADS, HD).transpose(1, 0, 2)

    def one_head(items):
        query_head, key_head, value_head, largest, denominator, summed = items
        scores = (
            jnp.einsum("gtd,pd->gtp", query_head, key_head, preferred_element_type=jnp.float32)
            * inv_scale
        )
        scores = jnp.where(allowed[None], scores, neg_big)
        new_largest = jnp.maximum(largest, jnp.max(scores, axis=-1))
        factor = jnp.exp(largest - new_largest)
        weights = jnp.where(allowed[None], jnp.exp(scores - new_largest[..., None]), 0.0)
        new_denominator = denominator * factor + jnp.sum(weights, axis=-1)
        added = jnp.einsum(
            "gtp,pd->gtd",
            weights.astype(jnp.bfloat16),
            value_head,
            preferred_element_type=jnp.float32,
        )
        return (new_largest, new_denominator, summed * factor[..., None] + added)

    largest = jnp.full((KV_HEADS, GROUP, row_count), neg_big, jnp.float32)
    denominator = jnp.zeros((KV_HEADS, GROUP, row_count), jnp.float32)
    summed = jnp.zeros((KV_HEADS, GROUP, row_count, HD), jnp.float32)
    largest, denominator, summed = lax.map(
        one_head, (queries, keys, values, largest, denominator, summed)
    )
    result = summed / denominator[..., None]
    return result.transpose(2, 0, 1, 3).reshape(row_count, HEADS * HD).astype(jnp.bfloat16)


def solution(mesh):
    return jax.shard_map(
        per_device,
        mesh=mesh,
        in_specs=(P(("dp", "ctx"), None), P(("dp", "ctx"), None), P(("dp", "ctx")), P("dp", "ctx")),
        out_specs=P(("dp", "ctx"), None),
        check_vma=False,
    )
```

profile of v0, /device:TPU:5, one launch (start us, length us, event | category | flops | bytes accessed | tf_op | source)
XLA Modules:
  0.0 231.1 jit_solution(9436826210657329006)
XLA Ops:
  6.5 0.0 copy-start
  6.5 0.0 copy-start.1
  6.5 0.8 add_select_fusion
  7.4 0.7 fusion.41
  8.1 1.2 reduce-window.6
  9.3 0.2 slice_reduce_fusion
  9.6 0.1 fusion.32
  9.7 0.7 compare_select_fusion.5
  10.4 2.4 %scatter_custom_fusion = s32[512]{0:T(512)S(1)} fusion(s32[512]{0:T(512)S(1)} %compare_select_fusion.5, s32[512]{0:T(512)S(1)} %iota.24, s32[]{:T(128)} %copy.40), kind=kCustom, calls=%fused_computation.70 | custom fusion | bytes 2052 | tf_op jit(solution)/shard_map/scatter | solution.py:28
  12.8 3.6 %gather_fusion.1 = s32[512]{0:T(512)S(1)} fusion(s32[512]{0:T(512)} %param.8, s32[1024]{0:T(1024)S(1)} %pad_clamp_fusion.1), kind=kCustom, calls=%fused_computation.1 | custom fusion | bytes 6144 | tf_op jit(solution)/shard_map/gather | solution.py:32
  16.5 0.7 all_to_all.27
  17.2 6.4 %all-to-all-start.1 = ((s32[32,16,1]{1,2,0:T(1,128)}), s32[32,16,1]{1,2,0:T(1,128)S(1)}, u32[]{:S(2)}, u32[]{:S(2)}) async-start(s32[32,16,1]{1,2,0:T(1,128)} %bitcast.4), calls=%async_computation.1 | async-start | bytes 32768 | tf_op jit(solution)/shard_map/all_to_all | solution.py:36
  23.6 0.0 copy-done.1
  23.6 2.8 %gather_fusion.3 = bf16[512,1024]{1,0:T(8,128)(2,1)} fusion(bf16[512,1024]{1,0:T(8,128)(2,1)S(1)} %copy-done.1, s32[1024]{0:T(1024)S(1)} %pad_clamp_fusion.1), kind=kCustom, calls=%fused_computation.3 | custom fusion | bytes 2099200 | tf_op jit(solution)/shard_map/gather | solution.py:31
  26.4 2.8 %all-to-all-done.1 = s32[32,16,1]{1,2,0:T(1,128)S(1)} async-done(((s32[32,16,1]{1,2,0:T(1,128)}), s32[32,16,1]{1,2,0:T(1,128)S(1)}, u32[]{:S(2)}, u32[]{:S(2)}) %all-to-all-start.1) | async-done | bytes 2080 | tf_op jit(solution)/shard_map/all_to_all | solution.py:36
  29.2 4.1 %all-to-all-start.2 = ((bf16[32,16,1024]{2,1,0:T(8,128)(2,1)}), bf16[32,16,1024]{2,1,0:T(8,128)(2,1)S(1)}, u32[]{:S(2)}, u32[]{:S(2)}) async-start(bf16[32,16,1024]{2,1,0:T(8,128)(2,1)} %bitcast.76), calls=%async_computation.2 | async-start | bytes 2097152 | tf_op jit(solution)/shard_map/all_to_all | solution.py:35
  33.3 0.0 all-gather.4.cloned.1.call-start
  33.3 0.6 broadcast.204
  33.9 0.7 reduce.5
  34.7 0.1 all_to_all.29
  34.8 2.4 %scatter_custom_fusion.1 = s32[512]{0:T(512)S(1)} fusion(s32[512]{0:T(512)S(1)} %bitcast.80, s32[512]{0:T(512)S(1)} %iota.25, s32[]{:T(128)} %copy.40), kind=kCustom, calls=%fused_computation.68 | custom fusion | bytes 2052 | tf_op jit(solution)/shard_map/scatter | solution.py:42
  37.2 22.3 %all-to-all-done.2 = bf16[32,16,1024]{2,1,0:T(8,128)(2,1)S(1)} async-done(((bf16[32,16,1024]{2,1,0:T(8,128)(2,1)}), bf16[32,16,1024]{2,1,0:T(8,128)(2,1)S(1)}, u32[]{:S(2)}, u32[]{:S(2)}) %all-to-all-start.2) | async-done | bytes 1048608 | tf_op jit(solution)/shard_map/all_to_all | solution.py:35
  59.6 2.8 %gather_fusion.4 = bf16[512,1024]{1,0:T(8,128)(2,1)} fusion(bf16[512,1024]{1,0:T(8,128)(2,1)S(1)} %bitcast.74, s32[1024]{0:T(1024)S(1)} %pad_clamp_fusion), kind=kCustom, calls=%fused_computation.4 | custom fusion | bytes 2099200 | tf_op jit(solution)/shard_map/gather | solution.py:44
  62.4 0.0 all-gather.4.cloned.1.call-update
  62.4 0.0 copy-done
  62.4 3.3 %gather_fusion = bf16[512,2048]{1,0:T(8,128)(2,1)} fusion(bf16[512,2048]{1,0:T(8,128)(2,1)S(1)} %copy-done, s32[1024]{0:T(1024)S(1)} %pad_clamp_fusion.1), kind=kCustom, calls=%fused_computation | custom fusion | bytes 4196352 | tf_op jit(solution)/shard_map/gather | solution.py:30
  65.7 0.0 copy-start.2
  65.7 3.7 %all-to-all-start = ((bf16[32,16,2048]{2,1,0:T(8,128)(2,1)}), bf16[32,16,2048]{2,1,0:T(8,128)(2,1)}, u32[]{:S(2)}, u32[]{:S(2)}) async-start(bf16[32,16,2048]{2,1,0:T(8,128)(2,1)} %bitcast.75), calls=%async_computation | async-start | bytes 4194304 | tf_op jit(solution)/shard_map/all_to_all | solution.py:34
  69.4 0.0 copy-done.2
  69.4 27.3 %all-gather = s32[1,2048]{1,0:T(1,128)S(1)} all-gather(s32[1,512]{1,0:T(1,128)S(1)} %copy-done.2), channel_id=2, replica_groups=mesh['dp'=8,'ctx'=4] {'ctx'}, dimensions={1}, use_global_device_ids=true | all-gather | bytes 10240 | tf_op jit(solution)/shard_map/all_gather | solution.py:55
  96.7 20.9 %all-to-all-done = bf16[32,16,2048]{2,1,0:T(8,128)(2,1)} async-done(((bf16[32,16,2048]{2,1,0:T(8,128)(2,1)}), bf16[32,16,2048]{2,1,0:T(8,128)(2,1)}, u32[]{:S(2)}, u32[]{:S(2)}) %all-to-all-start) | async-done | bytes 2097184 | tf_op jit(solution)/shard_map/all_to_all | solution.py:34
  117.6 7.1 %gather_fusion.2 = bf16[512,2048]{1,0:T(8,128)(2,1)} fusion(bf16[512,2048]{1,0:T(8,128)(2,1)} %bitcast.3, s32[1024]{0:T(1024)S(1)} %pad_clamp_fusion), kind=kCustom, calls=%fused_computation.2 | custom fusion | bytes 4196352 | tf_op jit(solution)/shard_map/gather | solution.py:44
  124.7 4.5 %reshape.143 = bf16[512,4,4,128]{3,2,1,0:T(4,128)(2,1)} reshape(bf16[512,2048]{1,0:T(8,128)(2,1)} %gather_fusion.2) | data formatting | bytes 4194304 | tf_op jit(solution)/shard_map/reshape | solution.py:53
  129.2 3.5 %copy.27 = bf16[512,4,4,128]{3,0,2,1:T(8,128)(2,1)} copy(bf16[512,4,4,128]{3,2,1,0:T(4,128)(2,1)} %reshape.143) | data formatting | bytes 4194304 | tf_op jit(solution)/shard_map/reshape | solution.py:53
  132.6 2.2 all-gather.4.cloned.1.call-done
  134.9 2.9 %slice_bitcast_fusion = (bf16[256,4,8,128]{3,2,1,0:T(8,128)(2,1)S(1)}, bf16[256,4,8,128]{3,2,1,0:T(8,128)(2,1)S(1)}) fusion(bf16[2048,1024]{1,0:T(8,128)(2,1)} %all-gather.4.cloned.1.call-done), kind=kLoop, calls=%fused_computation.38 | loop fusion | bytes 8388608
  137.8 2.8 %bitcast_bitcast_fusion = (bf16[4,2048,128]{2,1,0:T(8,128)(2,1)}, bf16[4,2048,128]{2,1,0:T(8,128)(2,1)}) fusion(bf16[256,4,8,128]{3,2,1,0:T(8,128)(2,1)S(1)} %get-tuple-element.90, bf16[256,4,8,128]{3,2,1,0:T(8,128)(2,1)S(1)} %get-tuple-element.91), kind=kLoop, calls=%fused_computation.36 | loop fusion | bytes 8388608 | tf_op jit(solution)/shard_map/transpose | solution.py:60
  140.6 73.4 %while.13 = (s32[]{:T(128)}, f32[4,4,512]{2,1,0:T(4,128)S(1)}, f32[4,4,512,128]{3,2,1,0:T(8,128)}, bf16[4,4,512,128]{3,2,1,0:T(8,128)(2,1)}, bf16[4,2048,128]{2,...) while((s32[]{:T(128)}, f32[4,4,512]{2,1,0:T(4,128)S(1)}, ...), condition=%wide.region_8.9_spmd.clone, body=%wide.region_5.8_spmd.clone.sunk | while | flops 2205427712 | bytes 57251952 | solution.py:84
  140.6 1.2 fusion.50
  141.8 4.8 %fusion.51 = (f32[4,512]{1,0:T(4,128)S(1)}, f32[4,512,2048]{2,1,0:T(8,128)S(1)}) fusion(pred[512,2048]{1,0:T(8,128)(4,1)S(1)} %fusion.50, bf16[4,2048,128]{2,1,0:T(8,128)(2,1)} %get-tuple-element.181, s32[]{:T(128)S(6)} %copy.33, bf16[4,4,512,128]{3,2,1,0:T(8,128)(2,1)} %get-tuple-element.180), kind=kOutput, calls=%fused_computation.10.clone.1 | convolution fusion | flops 1086322688 | bytes 18883584 | tf_op jit(solution)/shard_map/while/body/eval_jaxpr/gtd,pd->gtp/dot_general | solution.py:65
  146.6 5.0 %fusion.52 = f32[4,512]{1,0:T(4,128)S(1)} fusion(f32[4,512,2048]{2,1,0:T(8,128)S(1)} %get-tuple-element.153, f32[4,512]{1,0:T(4,128)S(1)} %get-tuple-element.155, pred[512,2048]{1,0:T(8,128)(4,1)S(1)} %fusion.50), kind=kLoop, calls=%fused_computation.12.clone.1 | loop fusion | flops 20969472 | bytes 17842176 | tf_op jit(solution)/shard_map/while/body/eval_jaxpr/reduce_sum | solution.py:72
  151.6 7.3 %fusion.53 = f32[4,4,512,128]{3,2,1,0:T(8,128)} fusion(f32[4,4,512,128]{3,2,1,0:T(8,128)} %get-tuple-element.169, s32[]{:T(128)S(6)} %copy.33, f32[4,512,2048]{2,1,0:T(8,128)S(1)} %get-tuple-element.153, f32[4,512]{1,0:T(4,128)S(1)} %get-tuple-element.155, pred[512,2048]{1,0:T(8,128)(4,1)S(1)} %fusion.50, ...), kind=kOutput, calls=%fused_computation.19.clone.1 | convolution fusion | flops 1094975488 | bytes 19416064 | tf_op jit(solution)/shard_map/while/body/eval_jaxpr/gtp,pd->gtd/dot_general | solution.py:73
  158.9 1.2 fusion.50
  160.1 4.8 %fusion.51 = (f32[4,512]{1,0:T(4,128)S(1)}, f32[4,512,2048]{2,1,0:T(8,128)S(1)}) fusion(pred[512,2048]{1,0:T(8,128)(4,1)S(1)} %fusion.50, bf16[4,2048,128]{2,1,0:T(8,128)(2,1)} %get-tuple-element.181, s32[]{:T(128)S(6)} %copy.33, bf16[4,4,512,128]{3,2,1,0:T(8,128)(2,1)} %get-tuple-element.180), kind=kOutput, calls=%fused_computation.10.clone.1 | convolution fusion | flops 1086322688 | bytes 18883584 | tf_op jit(solution)/shard_map/while/body/eval_jaxpr/gtd,pd->gtp/dot_general | solution.py:65
  164.9 5.0 %fusion.52 = f32[4,512]{1,0:T(4,128)S(1)} fusion(f32[4,512,2048]{2,1,0:T(8,128)S(1)} %get-tuple-element.153, f32[4,512]{1,0:T(4,128)S(1)} %get-tuple-element.155, pred[512,2048]{1,0:T(8,128)(4,1)S(1)} %fusion.50), kind=kLoop, calls=%fused_computation.12.clone.1 | loop fusion | flops 20969472 | bytes 17842176 | tf_op jit(solution)/shard_map/while/body/eval_jaxpr/reduce_sum | solution.py:72
  170.0 7.3 %fusion.53 = f32[4,4,512,128]{3,2,1,0:T(8,128)} fusion(f32[4,4,512,128]{3,2,1,0:T(8,128)} %get-tuple-element.169, s32[]{:T(128)S(6)} %copy.33, f32[4,512,2048]{2,1,0:T(8,128)S(1)} %get-tuple-element.153, f32[4,512]{1,0:T(4,128)S(1)} %get-tuple-element.155, pred[512,2048]{1,0:T(8,128)(4,1)S(1)} %fusion.50, ...), kind=kOutput, calls=%fused_computation.19.clone.1 | convolution fusion | flops 1094975488 | bytes 19416064 | tf_op jit(solution)/shard_map/while/body/eval_jaxpr/gtp,pd->gtd/dot_general | solution.py:73
  177.3 1.2 fusion.50
  178.5 4.8 %fusion.51 = (f32[4,512]{1,0:T(4,128)S(1)}, f32[4,512,2048]{2,1,0:T(8,128)S(1)}) fusion(pred[512,2048]{1,0:T(8,128)(4,1)S(1)} %fusion.50, bf16[4,2048,128]{2,1,0:T(8,128)(2,1)} %get-tuple-element.181, s32[]{:T(128)S(6)} %copy.33, bf16[4,4,512,128]{3,2,1,0:T(8,128)(2,1)} %get-tuple-element.180), kind=kOutput, calls=%fused_computation.10.clone.1 | convolution fusion | flops 1086322688 | bytes 18883584 | tf_op jit(solution)/shard_map/while/body/eval_jaxpr/gtd,pd->gtp/dot_general | solution.py:65
  183.2 5.0 %fusion.52 = f32[4,512]{1,0:T(4,128)S(1)} fusion(f32[4,512,2048]{2,1,0:T(8,128)S(1)} %get-tuple-element.153, f32[4,512]{1,0:T(4,128)S(1)} %get-tuple-element.155, pred[512,2048]{1,0:T(8,128)(4,1)S(1)} %fusion.50), kind=kLoop, calls=%fused_computation.12.clone.1 | loop fusion | flops 20969472 | bytes 17842176 | tf_op jit(solution)/shard_map/while/body/eval_jaxpr/reduce_sum | solution.py:72
  188.3 7.3 %fusion.53 = f32[4,4,512,128]{3,2,1,0:T(8,128)} fusion(f32[4,4,512,128]{3,2,1,0:T(8,128)} %get-tuple-element.169, s32[]{:T(128)S(6)} %copy.33, f32[4,512,2048]{2,1,0:T(8,128)S(1)} %get-tuple-element.153, f32[4,512]{1,0:T(4,128)S(1)} %get-tuple-element.155, pred[512,2048]{1,0:T(8,128)(4,1)S(1)} %fusion.50, ...), kind=kOutput, calls=%fused_computation.19.clone.1 | convolution fusion | flops 1094975488 | bytes 19416064 | tf_op jit(solution)/shard_map/while/body/eval_jaxpr/gtp,pd->gtd/dot_general | solution.py:73
  195.6 1.2 fusion.50
  196.8 4.8 %fusion.51 = (f32[4,512]{1,0:T(4,128)S(1)}, f32[4,512,2048]{2,1,0:T(8,128)S(1)}) fusion(pred[512,2048]{1,0:T(8,128)(4,1)S(1)} %fusion.50, bf16[4,2048,128]{2,1,0:T(8,128)(2,1)} %get-tuple-element.181, s32[]{:T(128)S(6)} %copy.33, bf16[4,4,512,128]{3,2,1,0:T(8,128)(2,1)} %get-tuple-element.180), kind=kOutput, calls=%fused_computation.10.clone.1 | convolution fusion | flops 1086322688 | bytes 18883584 | tf_op jit(solution)/shard_map/while/body/eval_jaxpr/gtd,pd->gtp/dot_general | solution.py:65
  201.6 5.0 %fusion.52 = f32[4,512]{1,0:T(4,128)S(1)} fusion(f32[4,512,2048]{2,1,0:T(8,128)S(1)} %get-tuple-element.153, f32[4,512]{1,0:T(4,128)S(1)} %get-tuple-element.155, pred[512,2048]{1,0:T(8,128)(4,1)S(1)} %fusion.50), kind=kLoop, calls=%fused_computation.12.clone.1 | loop fusion | flops 20969472 | bytes 17842176 | tf_op jit(solution)/shard_map/while/body/eval_jaxpr/reduce_sum | solution.py:72
  206.6 7.3 %fusion.53 = f32[4,4,512,128]{3,2,1,0:T(8,128)} fusion(f32[4,4,512,128]{3,2,1,0:T(8,128)} %get-tuple-element.169, s32[]{:T(128)S(6)} %copy.33, f32[4,512,2048]{2,1,0:T(8,128)S(1)} %get-tuple-element.153, f32[4,512]{1,0:T(4,128)S(1)} %get-tuple-element.155, pred[512,2048]{1,0:T(8,128)(4,1)S(1)} %fusion.50, ...), kind=kOutput, calls=%fused_computation.19.clone.1 | convolution fusion | flops 1094975488 | bytes 19416064 | tf_op jit(solution)/shard_map/while/body/eval_jaxpr/gtp,pd->gtd/dot_general | solution.py:73
  214.0 2.9 %fusion.30 = bf16[512,4,4,128]{3,0,2,1:T(8,128)(2,1)S(1)} fusion(f32[4,4,512,128]{3,2,1,0:T(8,128)} %get-tuple-element.43, f32[4,4,512]{2,1,0:T(4,128)S(1)} %get-tuple-element.44), kind=kLoop, calls=%fused_computation.41 | loop fusion | flops 2097152 | bytes 6324224 | tf_op jit(solution)/shard_map/convert_element_type | solution.py:88
  216.8 3.0 %copy.19 = bf16[512,4,4,128]{3,2,1,0:T(4,128)(2,1)} copy(bf16[512,4,4,128]{3,0,2,1:T(8,128)(2,1)S(1)} %fusion.30) | data formatting | bytes 4194304 | tf_op jit(solution)/shard_map/convert_element_type | solution.py:88
  219.8 4.5 %convert_element_type.20 = bf16[512,2048]{1,0:T(8,128)(2,1)} reshape(bf16[512,4,4,128]{3,2,1,0:T(4,128)(2,1)} %copy.19) | data formatting | bytes 4194304 | tf_op jit(solution)/shard_map/convert_element_type | solution.py:88
  (21 shorter events, 0.2 us)
Async XLA Ops:
  6.5 55.9 %copy-start = (bf16[512,2048]{1,0:T(8,128)(2,1)S(1)}, bf16[512,2048]{1,0:T(8,128)(2,1)}, u32[]{:S(2)}) copy-start(bf16[512,2048]{1,0:T(8,128)(2,1)} %param.6) | copy-start | bytes 6291460
  6.5 17.0 %copy-start.1 = (bf16[512,1024]{1,0:T(8,128)(2,1)S(1)}, bf16[512,1024]{1,0:T(8,128)(2,1)}, u32[]{:S(2)}) copy-start(bf16[512,1024]{1,0:T(8,128)(2,1)} %param.7) | copy-start | bytes 3145732
  17.2 12.0 %all-to-all-start.1 = ((s32[32,16,1]{1,2,0:T(1,128)}), s32[32,16,1]{1,2,0:T(1,128)S(1)}, u32[]{:S(2)}, u32[]{:S(2)}) async-start(s32[32,16,1]{1,2,0:T(1,128)} %bitcast.4), calls=%async_computation.1 | async-start | bytes 32768 | tf_op jit(solution)/shard_map/all_to_all | solution.py:36
  29.2 30.4 %all-to-all-start.2 = ((bf16[32,16,1024]{2,1,0:T(8,128)(2,1)}), bf16[32,16,1024]{2,1,0:T(8,128)(2,1)S(1)}, u32[]{:S(2)}, u32[]{:S(2)}) async-start(bf16[32,16,1024]{2,1,0:T(8,128)(2,1)} %bitcast.76), calls=%async_computation.2 | async-start | bytes 2097152 | tf_op jit(solution)/shard_map/all_to_all | solution.py:35
  33.3 101.6 %all-gather.4.cloned.1.call-start = ((), (), s32[]{:S(2)}) async-start(), calls=%async_computation.3 | async-start | bytes 5242880 | tf_op jit(solution)/shard_map/all_gather | solution.py:54
  65.7 3.7 %copy-start.2 = (s32[1,512]{1,0:T(1,128)S(1)}, s32[1,512]{1,0:T(1,128)}, u32[]{:S(2)}) copy-start(s32[1,512]{1,0:T(1,128)} %param.9) | copy-start | bytes 6148
  65.7 52.0 %all-to-all-start = ((bf16[32,16,2048]{2,1,0:T(8,128)(2,1)}), bf16[32,16,2048]{2,1,0:T(8,128)(2,1)}, u32[]{:S(2)}, u32[]{:S(2)}) async-start(bf16[32,16,2048]{2,1,0:T(8,128)(2,1)} %bitcast.75), calls=%async_computation | async-start | bytes 4194304 | tf_op jit(solution)/shard_map/all_to_all | solution.py:34
Sparse Core Ops, SparseCore 0:
  62.5 72.3 all-gather.3
where the time goes:
time: 234 us; the launch traced here: 231 us
  waiting for transfers between devices  48.3 us (21%)
  matrix products  48.3 us (21%)
  local copies, waits for them, and re-layouts  47.1 us (20%)
  other arithmetic  32.2 us (14%)
  blocking collectives  27.3 us (12%)
  starting transfers between devices  14.2 us (6%)
  between operations  13.6 us (6%)
    dot_general x4, matrix products, one_head(): jnp.einsum('gtp,pd->gtd', weights.astype(jnp.bfloat16), value_head, prefe...  29.2 us
    all_gather x1, blocking collectives, per_device(): doc_block = lax.all_gather(query_docs, 'ctx', axis=0, tiled=True)  27.3 us
    all_to_all x1, waiting for transfers between devices, arrange(): lax.all_to_all(kv_send, ('dp', 'ctx'), split_axis=0, concat_axis=0, tiled...  22.3 us
    all_to_all x1, waiting for transfers between devices, arrange(): lax.all_to_all(q_send, ('dp', 'ctx'), split_axis=0, concat_axis=0, tiled=...  20.9 us
    reduce_sum x4, other arithmetic, one_head(): new_denominator = denominator * factor + jnp.sum(weights, axis=-1)  20.1 us
    dot_general x4, matrix products, one_head(): jnp.einsum('gtd,pd->gtp', query_head, key_head, preferred_element_type=jn...  19 us
    gather x2, local copies, waits for them, and re-layouts, arrange(): return (got_q[inverse], got_kv[inverse])  9.87 us
    reshape x2, local copies, waits for them, and re-layouts, per_device(): q_here.reshape(row_count, KV_HEADS, GROUP, HD).transpose(1, 2, 0, 3)  7.92 us
  transfers between devices with their start and end apart: 4, of which 4 were waited for; matrix products, arithmetic and copies ran while one was open for 11% of the time, Pallas kernels for 0%

commit v1 on v0

v1 whole, which is shorter than its diff:
```python
import functools
import math

import jax
import jax.numpy as jnp
from jax import lax
from jax.experimental import pallas as pl
from jax.experimental.pallas import tpu as pltpu
from jax.sharding import PartitionSpec as P

HEADS = 16
KV_HEADS = 4
HD = 128
GROUP = 4
KV_COLS = 2 * KV_HEADS * HD
GROUP_COLS = GROUP * HD
META = 128
Q_TILE = 128
K_STEP = 256
NEG = -1e30
MIB = 1 << 20

F32 = jnp.float32
BF16 = jnp.bfloat16


def dot(a, b):
    return jnp.dot(a, b, preferred_element_type=F32)


def dot_nt(a, b):
    return lax.dot_general(a, b, (((1,), (1,)), ((), ())), preferred_element_type=F32)


def iota(shape, dim):
    return lax.broadcasted_iota(jnp.int32, shape, dim)


def send_matrix(slot, devices):
    rows = slot.shape[1]
    target = slot // rows
    one_hot = (iota((devices, rows), 0) == target).astype(F32)
    before = (iota((rows, rows), 0) < iota((rows, rows), 1)).astype(BF16)
    rank = jnp.sum(dot(one_hot.astype(BF16), before) * one_hot, axis=0, keepdims=True)
    where_to = target * (rows // devices) + rank.astype(jnp.int32)
    return (iota((rows, rows), 0) == where_to).astype(BF16)


def pack_kv_kernel(devices, slot_ref, kv_ref, out_ref):
    slot = slot_ref[...]
    rows = slot.shape[1]
    matrix = send_matrix(slot, devices)
    local = slot % rows
    which = iota((META, rows), 0)
    digits = jnp.where(which == 0, local // 16, jnp.where(which == 1, local % 16, 0))
    out_ref[:, :KV_COLS] = dot(matrix, kv_ref[...]).astype(BF16)
    out_ref[:, KV_COLS:] = dot_nt(matrix, digits.astype(BF16)).astype(BF16)


def pack_q_kernel(devices, slot_ref, q_ref, out_ref, matrix_ref):
    @pl.when(pl.program_id(0) == 0)
    def _():
        matrix_ref[...] = send_matrix(slot_ref[...], devices)

    out_ref[...] = dot(matrix_ref[...], q_ref[...]).astype(BF16)


def sort_kv_kernel(got_ref, out_ref, place_ref):
    rows = got_ref.shape[0]
    pick = (iota((8, META), 0) == iota((8, META), 1)).astype(BF16)
    digits = dot_nt(pick, got_ref[:, KV_COLS:])
    place = (digits[0:1] * 16 + digits[1:2]).astype(jnp.int32)
    place_ref[...] = place
    matrix = (iota((rows, rows), 0) == place).astype(BF16)
    out_ref[...] = dot(matrix, got_ref[:, :KV_COLS]).astype(BF16)


def attend_kernel(blocks, steps_ref, place_ref, start_ref, q_ref, *refs):
    key_refs, value_refs = refs[:blocks], refs[blocks : 2 * blocks]
    out_ref, matrix_ref, bias_ref, q_buf, key_buf, value_buf = refs[2 * blocks :]
    rows = q_ref.shape[0]
    width = key_buf.shape[0]
    pad = width - blocks * rows
    scale = math.log2(math.e) / math.sqrt(HD)

    @pl.when(pl.program_id(0) == 0)
    def _():
        matrix_ref[...] = (iota((rows, rows), 0) == place_ref[...]).astype(BF16)
        column = iota((rows, width), 1)
        last = iota((rows, 1), 0) + (width - rows)
        allowed = (column >= start_ref[...] + pad) & (column <= last)
        bias_ref[...] = jnp.where(allowed, 0.0, NEG)
        key_buf[:pad, :] = jnp.zeros((pad, HD), BF16)
        value_buf[:pad, :HD] = jnp.zeros((pad, HD), BF16)
        value_buf[:, HD:] = jnp.ones((width, HD), BF16)

    q_buf[...] = dot(matrix_ref[...], q_ref[...]).astype(BF16)
    for b in range(blocks):
        key_buf[pl.ds(pad + b * rows, rows), :] = key_refs[b][...]
        value_buf[pl.ds(pad + b * rows, rows), :HD] = value_refs[b][...]

    @pl.loop(0, rows // Q_TILE)
    def _(tile):
        here = pl.ds(pl.multiple_of(tile * Q_TILE, Q_TILE), Q_TILE)
        end = (width - rows) + (tile + 1) * Q_TILE

        def run(steps):
            span = steps * K_STEP
            keys = pl.ds(pl.multiple_of(end - span, Q_TILE), span)
            bias = bias_ref[here, keys]
            queries = jnp.concatenate(
                [q_buf[here, h * HD : (h + 1) * HD] for h in range(GROUP)], axis=0
            )
            scores = dot_nt(queries, key_buf[keys, :])
            scores = scores.reshape(GROUP, Q_TILE, span) + bias[None]
            largest = jnp.max(scores, axis=-1, keepdims=True)
            probs = jnp.exp2((scores - largest) * scale).astype(BF16)
            summed = dot(probs.reshape(GROUP * Q_TILE, span), value_buf[keys, :])
            result = (summed[:, :HD] / summed[:, HD:]).astype(BF16)
            for h in range(GROUP):
                out_ref[here, h * HD : (h + 1) * HD] = result[h * Q_TILE : (h + 1) * Q_TILE]

        for steps in range(1, -(-(width - pad) // K_STEP) + 1):
            pl.when(steps_ref[tile] == steps)(functools.partial(run, steps))


def all_to_all(x):
    return lax.all_to_all(x, ("dp", "ctx"), split_axis=0, concat_axis=0, tiled=True)


def per_device(q_rows, kv_rows, packed_slot, doc_ids):
    rows = q_rows.shape[0]
    ctx_size = lax.axis_size("ctx")
    devices = lax.axis_size("dp") * ctx_size
    pack = rows * ctx_size
    doc_max = pack // 2
    before = min(ctx_size - 1, -(-(doc_max - 1) // rows))
    blocks = before + 1
    slot = packed_slot.reshape(1, rows)
    params = pltpu.CompilerParams(vmem_limit_bytes=48 * MIB)

    kv_out = pl.pallas_call(
        functools.partial(pack_kv_kernel, devices),
        out_shape=jax.ShapeDtypeStruct((rows, KV_COLS + META), BF16),
        compiler_params=params,
        name="pack_kv",
    )(slot, kv_rows)
    kv_got = all_to_all(kv_out)

    q_out = pl.pallas_call(
        functools.partial(pack_q_kernel, devices),
        out_shape=jax.ShapeDtypeStruct(q_rows.shape, BF16),
        grid=(KV_HEADS,),
        in_specs=[
            pl.BlockSpec((1, rows), lambda g: (0, 0)),
            pl.BlockSpec((rows, GROUP_COLS), lambda g: (0, g)),
        ],
        out_specs=pl.BlockSpec((rows, GROUP_COLS), lambda g: (0, g)),
        scratch_shapes=[pltpu.VMEM((rows, rows), BF16)],
        compiler_params=params,
        name="pack_q",
    )(slot, q_rows)
    q_got = all_to_all(q_out)

    kv_here, place = pl.pallas_call(
        sort_kv_kernel,
        out_shape=(
            jax.ShapeDtypeStruct((rows, KV_COLS), BF16),
            jax.ShapeDtypeStruct((1, rows), jnp.int32),
        ),
        compiler_params=params,
        name="sort_kv",
    )(kv_got)

    def from_before(x, distance):
        return lax.ppermute(x, "ctx", [(i, i + distance) for i in range(ctx_size - distance)])

    docs = doc_ids.reshape(rows) + 1
    doc_line = jnp.concatenate([from_before(docs, d) for d in range(before, 0, -1)] + [docs])
    start = jnp.sum((doc_line[None, :] < docs[:, None]).astype(jnp.int32), axis=1)
    ends = before * rows + jnp.arange(Q_TILE, rows + 1, Q_TILE, dtype=jnp.int32)
    steps = (ends - start[::Q_TILE] + K_STEP - 1) // K_STEP

    kv_blocks = [from_before(kv_here, d) for d in range(before, 0, -1)] + [kv_here]

    width = Q_TILE + blocks * rows
    whole = lambda shape: pl.BlockSpec(shape, lambda g, s: (0, 0))
    return pl.pallas_call(
        functools.partial(attend_kernel, blocks),
        out_shape=jax.ShapeDtypeStruct(q_rows.shape, BF16),
        grid_spec=pltpu.PrefetchScalarGridSpec(
            num_scalar_prefetch=1,
            grid=(KV_HEADS,),
            in_specs=[whole((1, rows)), whole((rows, 1))]
            + [pl.BlockSpec((rows, GROUP_COLS), lambda g, s: (0, g))]
            + [pl.BlockSpec((rows, HD), lambda g, s: (0, g))] * blocks
            + [pl.BlockSpec((rows, HD), lambda g, s: (0, KV_HEADS + g))] * blocks,
            out_specs=pl.BlockSpec((rows, GROUP_COLS), lambda g, s: (0, g)),
            scratch_shapes=[
                pltpu.VMEM((rows, rows), BF16),
                pltpu.VMEM((rows, width), F32),
                pltpu.VMEM((rows, GROUP_COLS), BF16),
                pltpu.VMEM((width, HD), BF16),
                pltpu.VMEM((width, 2 * HD), BF16),
            ],
        ),
        compiler_params=params,
        name="attend",
    )(steps, place, start.reshape(rows, 1), q_got, *kv_blocks, *kv_blocks)


def solution(mesh):
    return jax.shard_map(
        per_device,
        mesh=mesh,
        in_specs=(P(("dp", "ctx"), None), P(("dp", "ctx"), None), P(("dp", "ctx")), P("dp", "ctx")),
        out_specs=P(("dp", "ctx"), None),
        check_vma=False,
    )
```

time: 234 us -> 140 us (0.60)
  matrix products: 48.3 us -> 0 us
  local copies, waits for them, and re-layouts: 47.1 us -> 2.16 us
  waiting for transfers between devices: 48.3 us -> 84.7 us
  Pallas kernels: 0 us -> 33.8 us
  other arithmetic: 32.2 us -> 0.51 us
  blocking collectives: 27.3 us -> 0 us
  between operations: 13.6 us -> 0.13 us
  starting transfers between devices: 14.2 us -> 17.7 us
    ppermute x0 -> x4, waiting for transfers between devices: none -> 59.2 us  [from_before(): lax.ppermute(x, 'ctx', [(i, i + distance) for i in range(ctx_size - dista...]
    dot_general x8 -> x0, matrix products: 48.3 us -> none  [the longest x4 29.2 us: one_head(): jnp.einsum('gtp,pd->gtd', weights.astype(jnp.bfloat16), value_head, prefe...]
    pallas_call x0 -> x4, Pallas kernels: none -> 33.8 us  [the longest x1 26.4 us: per_device(): pl.pallas_call(functools.partial(attend_kernel, blocks), out_shape=jax.Sh...]
    all_gather x1 -> x0, blocking collectives: 27.3 us -> none  [per_device(): doc_block = lax.all_gather(query_docs, 'ctx', axis=0, tiled=True)]
    all_to_all x3 -> x2, waiting for transfers between devices: 46.1 us -> 25.5 us  [all_to_all(): lax.all_to_all(x, ('dp', 'ctx'), split_axis=0, concat_axis=0, tiled=True)]
    reduce_sum x5 -> x1, other arithmetic: 20.2 us -> 0.49 us  [per_device(): jnp.sum((doc_line[None, :] < docs[:, None]).astype(jnp.int32), axis=1)]
    gather x5 -> x0, local copies, waits for them, and re-layouts: 19.6 us -> none  [the longest x2 9.87 us: arrange(): return (got_q[inverse], got_kv[inverse])]
    reshape x2 -> x1, local copies, waits for them, and re-layouts: 7.92 us -> 0.15 us  [per_device(): start.reshape(rows, 1)]
  transfers between devices with their start and end apart: 4 -> 6, of which waited for: 4 -> 3; matrix products, arithmetic and copies ran while one was open for 11% -> 1% of each run, Pallas kernels for 0% -> 4%
where the time goes in v1:
time: 140 us; the launch traced here: 139 us
  waiting for transfers between devices  84.7 us (60%)
  Pallas kernels  33.8 us (24%)
  starting transfers between devices  17.7 us (13%)
  local copies, waits for them, and re-layouts  2.16 us (2%)
    ppermute x4, waiting for transfers between devices, from_before(): lax.ppermute(x, 'ctx', [(i, i + distance) for i in range(ctx_size - dista...  59.2 us
    pallas_call x1, Pallas kernels, per_device(): pl.pallas_call(functools.partial(attend_kernel, blocks), out_shape=jax.Sh...  26.4 us
    all_to_all x2, waiting for transfers between devices, all_to_all(): lax.all_to_all(x, ('dp', 'ctx'), split_axis=0, concat_axis=0, tiled=True)  25.5 us
    all_to_all x2, starting transfers between devices, all_to_all(): lax.all_to_all(x, ('dp', 'ctx'), split_axis=0, concat_axis=0, tiled=True)  10.1 us
    ppermute x4, starting transfers between devices, from_before(): lax.ppermute(x, 'ctx', [(i, i + distance) for i in range(ctx_size - dista...  7.59 us
    pallas_call x1, Pallas kernels, per_device(): pl.pallas_call(functools.partial(pack_q_kernel, devices), out_shape=jax.S...  3.48 us
  transfers between devices with their start and end apart: 6, of which 3 were waited for; matrix products, arithmetic and copies ran while one was open for 1% of the time, Pallas kernels for 4%

profile of v1, /device:TPU:5, one launch (start us, length us, event | category | flops | bytes accessed | tf_op | source)
XLA Modules:
  0.0 139.0 jit_solution(11569764219935279900)
XLA Ops:
  0.0 0.0 copy-start.1
  0.0 1.2 copy-done.1
  1.2 0.0 copy-start.2
  1.2 0.7 copy-done.2
  1.9 0.0 copy-start
  1.9 0.0 copy-start.3
  1.9 2.1 %pack_kv.1 = bf16[512,1152]{1,0:T(8,128)(2,1)} custom-call(s32[1,512]{1,0:T(1,128)S(1)} %bitcast.9, bf16[512,1024]{1,0:T(8,128)(2,1)S(1)} %copy-done.1), custom_call_target="tpu_custom_call" | custom-call | tf_op jit(solution)/shard_map/pack_kv/pallas_call | solution.py:142
  4.0 6.4 %all-to-all-start = ((bf16[32,16,1152]{2,1,0:T(8,128)(2,1)}), bf16[32,16,1152]{2,1,0:T(8,128)(2,1)S(1)}, u32[]{:S(2)}, u32[]{:S(2)}) async-start(bf16[32,16,1152]{2,1,0:T(8,128)(2,1)} %bitcast.2), calls=%async_computation | async-start | bytes 2359296 | tf_op jit(solution)/shard_map/all_to_all | solution.py:128
  10.4 0.0 copy-done
  10.4 0.0 copy-done.3
  10.4 3.5 %pack_q.1 = bf16[512,2048]{1,0:T(8,128)(2,1)} custom-call(s32[1,512]{1,0:T(1,128)S(1)} %bitcast.10, bf16[512,2048]{1,0:T(8,128)(2,1)S(1)} %copy-done), custom_call_target="tpu_custom_call" | custom-call | tf_op jit(solution)/shard_map/pack_q/pallas_call | solution.py:150
  13.9 25.5 %all-to-all-done = bf16[32,16,1152]{2,1,0:T(8,128)(2,1)S(1)} async-done(((bf16[32,16,1152]{2,1,0:T(8,128)(2,1)}), bf16[32,16,1152]{2,1,0:T(8,128)(2,1)S(1)}, u32[]{:S(2)}, u32[]{:S(2)}) %all-to-all-start) | async-done | bytes 1179680 | tf_op jit(solution)/shard_map/all_to_all | solution.py:128
  39.4 0.0 copy-start.4
  39.4 3.7 %all-to-all-start.1 = ((bf16[32,16,2048]{2,1,0:T(8,128)(2,1)}), bf16[32,16,2048]{2,1,0:T(8,128)(2,1)S(1)}, u32[]{:S(2)}, u32[]{:S(2)}) async-start(bf16[32,16,2048]{2,1,0:T(8,128)(2,1)} %bitcast.5), calls=%async_computation.1 | async-start | bytes 4194304 | tf_op jit(solution)/shard_map/all_to_all | solution.py:128
  43.1 1.8 %sort_kv.1 = (bf16[512,1024]{1,0:T(8,128)(2,1)}, s32[1,512]{1,0:T(1,128)S(1)}) custom-call(bf16[512,1152]{1,0:T(8,128)(2,1)S(1)} %bitcast.8), custom_call_target="tpu_custom_call" | custom-call | tf_op jit(solution)/shard_map/sort_kv/pallas_call | solution.py:165
  44.9 1.3 collective-permute-start.2
  46.2 3.1 %collective-permute-start.3 = (bf16[512,1024]{1,0:T(8,128)(2,1)}, bf16[512,1024]{1,0:T(8,128)(2,1)}, u32[]{:S(2)}, u32[]{:S(2)}) collective-permute-start(bf16[512,1024]{1,0:T(8,128)(2,1)} %get-tuple-element.8.refs_2_.refs_5_), channel_id=1, source_target_pairs={{0,1},{1,2},{2,3},{4,5},{5,6},{6,7},{8,9},{9,10},{10,11},{12,13},{... | collective-permute-start | bytes 3145736 | tf_op jit(solution)/shard_map/ppermute | solution.py:176
  49.3 0.0 copy-done.4
  49.3 1.9 %collective-permute-start.1 = (s32[512]{0:T(512)S(1)}, s32[512]{0:T(512)S(1)}, u32[]{:S(2)}, u32[]{:S(2)}) collective-permute-start(s32[512]{0:T(512)S(1)} %bitcast.11), channel_id=1, source_target_pairs={{0,1},{1,2},{2,3},{4,5},{5,6},{6,7},{8,9},{9,10},{10,11},{12,13},{... | collective-permute-start | bytes 6152 | tf_op jit(solution)/shard_map/ppermute | solution.py:176
  51.2 1.3 collective-permute-start
  52.5 40.9 %collective-permute-done.1 = s32[512]{0:T(512)S(1)} collective-permute-done((s32[512]{0:T(512)S(1)}, s32[512]{0:T(512)S(1)}, u32[]{:S(2)}, u32[]{:S(2)}) %collective-permute-start.1) | collective-permute-done | bytes 2080 | tf_op jit(solution)/shard_map/ppermute | solution.py:176
  93.4 18.3 %collective-permute-done = s32[512]{0:T(512)S(1)} collective-permute-done((s32[512]{0:T(512)S(1)}, s32[512]{0:T(512)S(1)}, u32[]{:S(2)}, u32[]{:S(2)}) %collective-permute-start) | collective-permute-done | bytes 2080 | tf_op jit(solution)/shard_map/ppermute | solution.py:176
  111.7 0.5 convert_reduce_fusion
  112.2 0.1 slice.3
  112.3 0.1 copy.6.start_ref
  112.5 0.0 collective-permute-done.2.refs_0_.refs_3_
  112.5 0.0 collective-permute-done.3.refs_1_.refs_4_
  112.5 0.0 all-to-all-done.1
  112.5 26.4 %attend.1 = bf16[512,2048]{1,0:T(8,128)(2,1)} custom-call(s32[4]{0:T(128)S(1)} %and_select_fusion.steps_ref, s32[1,512]{1,0:T(1,128)S(1)} %get-tuple-element.7.place_ref, s32[512,1]{1,0:T(8,128)S(1)} %copy.6.start_ref, bf16[512,2048]{1,0:T(8,128)(2,1)S(1)} %bitcast.7, bf16[512,1024]{1,0:T(8,128)(2,1)S(1)} %collective-permute-done.2.refs_0_.refs_3_, ...), custom_call_target="tpu_custom_call" | custom-call | tf_op jit(solution)/shard_map/attend/pallas_call | solution.py:188
  (3 shorter events, 0.0 us)
Async XLA Ops:
  0.0 1.2 copy-start.1
  1.2 0.7 copy-start.2
  1.9 8.5 %copy-start = (bf16[512,2048]{1,0:T(8,128)(2,1)S(1)}, bf16[512,2048]{1,0:T(8,128)(2,1)}, u32[]{:S(2)}) copy-start(bf16[512,2048]{1,0:T(8,128)(2,1)} %q_ref.1) | copy-start | bytes 6291460
  1.9 8.5 %copy-start.3 = (s32[512]{0:T(512)S(1)}, s32[512]{0:T(512)}, u32[]{:S(2)}) copy-start(s32[512]{0:T(512)} %param.6) | copy-start | bytes 6148
  4.0 35.4 %all-to-all-start = ((bf16[32,16,1152]{2,1,0:T(8,128)(2,1)}), bf16[32,16,1152]{2,1,0:T(8,128)(2,1)S(1)}, u32[]{:S(2)}, u32[]{:S(2)}) async-start(bf16[32,16,1152]{2,1,0:T(8,128)(2,1)} %bitcast.2), calls=%async_computation | async-start | bytes 2359296 | tf_op jit(solution)/shard_map/all_to_all | solution.py:128
  39.4 9.9 %copy-start.4 = (s32[1,512]{1,0:T(1,128)S(1)}, s32[1,512]{1,0:T(1,128)}, u32[]{:S(2)}) copy-start(s32[1,512]{1,0:T(1,128)} %param.7) | copy-start | bytes 6148
  39.4 73.2 %all-to-all-start.1 = ((bf16[32,16,2048]{2,1,0:T(8,128)(2,1)}), bf16[32,16,2048]{2,1,0:T(8,128)(2,1)S(1)}, u32[]{:S(2)}, u32[]{:S(2)}) async-start(bf16[32,16,2048]{2,1,0:T(8,128)(2,1)} %bitcast.5), calls=%async_computation.1 | async-start | bytes 4194304 | tf_op jit(solution)/shard_map/all_to_all | solution.py:128
  44.9 67.6 %collective-permute-start.2 = (bf16[512,1024]{1,0:T(8,128)(2,1)}, bf16[512,1024]{1,0:T(8,128)(2,1)S(1)}, u32[]{:S(2)}, u32[]{:S(2)}) collective-permute-start(bf16[512,1024]{1,0:T(8,128)(2,1)} %get-tuple-element.8.refs_2_.refs_5_), channel_id=1, source_target_pairs={{0,2},{1,3},{4,6},{5,7},{8,10},{9,11},{12,14},{13,15},{16,18},{17,... | collective-permute-start | bytes 3145736 | tf_op jit(solution)/shard_map/ppermute | solution.py:176
  46.2 66.3 %collective-permute-start.3 = (bf16[512,1024]{1,0:T(8,128)(2,1)}, bf16[512,1024]{1,0:T(8,128)(2,1)}, u32[]{:S(2)}, u32[]{:S(2)}) collective-permute-start(bf16[512,1024]{1,0:T(8,128)(2,1)} %get-tuple-element.8.refs_2_.refs_5_), channel_id=1, source_target_pairs={{0,1},{1,2},{2,3},{4,5},{5,6},{6,7},{8,9},{9,10},{10,11},{12,13},{... | collective-permute-start | bytes 3145736 | tf_op jit(solution)/shard_map/ppermute | solution.py:176
  49.3 44.1 %collective-permute-start.1 = (s32[512]{0:T(512)S(1)}, s32[512]{0:T(512)S(1)}, u32[]{:S(2)}, u32[]{:S(2)}) collective-permute-start(s32[512]{0:T(512)S(1)} %bitcast.11), channel_id=1, source_target_pairs={{0,1},{1,2},{2,3},{4,5},{5,6},{6,7},{8,9},{9,10},{10,11},{12,13},{... | collective-permute-start | bytes 6152 | tf_op jit(solution)/shard_map/ppermute | solution.py:176
  51.2 60.5 %collective-permute-start = (s32[512]{0:T(512)S(1)}, s32[512]{0:T(512)S(1)}, u32[]{:S(2)}, u32[]{:S(2)}) collective-permute-start(s32[512]{0:T(512)S(1)} %bitcast.12), channel_id=1, source_target_pairs={{0,2},{1,3},{4,6},{5,7},{8,10},{9,11},{12,14},{13,15},{16,18},{17,... | collective-permute-start | bytes 6152 | tf_op jit(solution)/shard_map/ppermute | solution.py:176
